TPU v7x, 128 devices: a whole 4x4x4 slice. The times are simulated.
128 devices in a mesh: dp: 4 (over z), expert: 32 (over y, x, core).
Axes of the slice: x: 4, y: 4, z: 4, core: 2. Of those that a mesh axis runs over, the one named last changes fastest.
Arguments:
- tokens: bfloat16 [4096, 4096], P('expert'), may hold values from -6 to 6
- expert_ids: int32 [4096, 8], P('expert'), may hold values from 0 to 63, all different within a row; in each aligned block of 128 rows (0 to 127, 128 to 255, ...) at most 32 rows name the same one
- gate_prob: float32 [4096, 8], P('expert'), may hold values from 0.02 to 0.3
- gate_weight: bfloat16 [64, 4096, 1536], P('expert', None, 'dp'), may hold values from -0.09375 to 0.09375
- up_weight: bfloat16 [64, 4096, 1536], P('expert', None, 'dp'), may hold values from -0.09375 to 0.09375
- tangent: bfloat16 [64, 1536, 4096], P('expert', None, 'dp'), may hold values from -0.15625 to 0.15625
- curvature: float32 [4096], P('dp'), may hold values from 0.1 to 1.9
Outputs:
- hessian_product: bfloat16 [64, 1536, 4096], P('expert', None, 'dp')
- tangent_image: bfloat16 [4096, 4096], P('expert', 'dp')
Inputs may be any that keep to these rules, and one draw needn't show every extreme that they name: `expert_ids`: each token names 8 different experts. Within each aligned block of 128 tokens no expert is named more than 32 times, and in every draw some expert is named exactly 32 times in some block.
All inputs are finite; a program needn't handle non-finite values.
Results may differ from a plain program's by a relative error of at most 0.007.
Values may be sent and summed in bfloat16 or wider, within the bound.
No kernel may reach another device: no remote copies, remote signals or barrier semaphores. Data moves between devices by JAX's collectives and lax.ppermute only.
A program may use at most 128 MiB of HBM per device.

v0:
```python
import jax
import jax.numpy as jnp
from jax import lax
from jax.sharding import PartitionSpec as P


def slot_of_rows(flat_ids, expert_total, capacity):
    onehot = (flat_ids[:, None] == jnp.arange(expert_total, dtype=jnp.int32)[None, :]).astype(
        jnp.int32
    )
    earlier = jnp.cumsum(onehot, axis=0, dtype=jnp.int32) - onehot
    position = jnp.sum(earlier * onehot, axis=1, dtype=jnp.int32)
    return flat_ids * capacity + position


def row_of_slots(slots, expert_total, capacity):
    row_total = slots.shape[0]
    empty_rows = jnp.full((expert_total * capacity,), row_total, jnp.int32)
    return empty_rows.at[slots].set(jnp.arange(row_total, dtype=jnp.int32))


def per_device(tokens, expert_ids, gate_prob, gate_weight, up_weight, tangent, curvature):
    token_count, width = tokens.shape
    top_count = expert_ids.shape[1]
    local_experts = gate_weight.shape[0]
    groups = lax.axis_size("expert")
    expert_total = local_experts * groups
    capacity = 2 * token_count * top_count // expert_total
    row_count = token_count * top_count
    quarter = tangent.shape[2]
    slots = slot_of_rows(expert_ids.reshape(row_count), expert_total, capacity)
    owners = row_of_slots(slots, expert_total, capacity)
    owner_tokens = owners // top_count
    shape_out = (groups, local_experts, capacity)
    padded = jnp.concatenate([tokens, jnp.zeros((1, width), tokens.dtype)], axis=0)
    outgoing = padded[owner_tokens].reshape(shape_out + (width,))
    arrived = lax.all_to_all(outgoing, "expert", split_axis=0, concat_axis=0, tiled=True)
    gate_pre = jnp.einsum(
        "sxcd,xdf->xscf", arrived, gate_weight, preferred_element_type=jnp.float32
    )
    up_pre = jnp.einsum("sxcd,xdf->xscf", arrived, up_weight, preferred_element_type=jnp.float32)
    hidden_share = (jax.nn.silu(gate_pre) * up_pre).astype(jnp.bfloat16)
    hidden = lax.all_gather(hidden_share, "dp", axis=3, tiled=True)
    expert_out = jnp.einsum(
        "xscf,xfd->sxcd", hidden, tangent, preferred_element_type=jnp.float32
    ).astype(jnp.bfloat16)
    returned = lax.all_to_all(expert_out, "expert", split_axis=0, concat_axis=0, tiled=True)
    per_row = returned.reshape(expert_total * capacity, quarter)[slots].reshape(
        token_count, top_count, quarter
    )
    combined = jnp.sum(gate_prob[:, :, None] * per_row.astype(jnp.float32), axis=1)
    tangent_image = combined.astype(jnp.bfloat16)
    weighted = curvature[None, :] * combined
    scaled = (gate_prob[:, :, None] * weighted[:, None, :]).reshape(row_count, quarter)
    padded_scaled = jnp.concatenate([scaled, jnp.zeros((1, quarter), jnp.float32)], axis=0)
    outgoing_scaled = padded_scaled[owners].astype(jnp.bfloat16).reshape(shape_out + (quarter,))
    incoming = lax.all_to_all(outgoing_scaled, "expert", split_axis=0, concat_axis=0, tiled=True)
    hessian_product = jnp.einsum(
        "xscf,sxcd->xfd", hidden, incoming, preferred_element_type=jnp.float32
    ).astype(jnp.bfloat16)
    return (hessian_product, tangent_image)


def solution(mesh):
    placed = (
        P("expert", None),
        P("expert", None),
        P("expert", None),
        P("expert", None, "dp"),
        P("expert", None, "dp"),
        P("expert", None, "dp"),
        P("dp"),
    )
    return jax.shard_map(
        per_device,
        mesh=mesh,
        in_specs=placed,
        out_specs=(P("expert", None, "dp"), P("expert", "dp")),
        check_vma=False,
    )
```

profile of v0, /device:TPU:1, one launch (start us, length us, event | category | flops | bytes accessed | tf_op | source)
XLA Modules:
  0.0 501.7 jit_solution(15067345853424834301)
XLA Ops:
  7.2 0.0 all-gather.2.cloned.1.call-start
  7.2 0.8 copy.23
  8.0 0.1 eq.29
  8.1 0.1 eq.25
  8.2 0.7 broadcast_multiply_fusion.1
  8.9 18.0 %reduce-window.6 = s32[64,8,128]{2,1,0:T(8,128)S(1)} reduce-window(s32[64,8,128]{2,1,0:T(8,128)S(1)} %fusion.19, s32[]{:T(128)} %constant.18.clone.1), window={size=1x1x128 pad=0_0x0_0x127_0}, to_apply=%region_0.0 | reduce-window | flops 8323072 | bytes 524292 | tf_op jit(solution)/shard_map/reduce-window
  26.9 0.1 slice.14
  27.0 0.1 copy.25
  27.2 0.1 copy.26
  27.3 0.1 broadcast_add_fusion
  27.5 0.1 copy.22
  27.6 0.1 mul.66
  27.7 0.1 fusion.18
  27.8 4.3 scatter_custom_fusion
  32.1 1.3 concatenate.6
  33.4 14.3 %gather_fusion = bf16[2048,4096]{1,0:T(8,128)(2,1)} fusion(bf16[129,4096]{1,0:T(8,128)(2,1)S(1)} %concatenate.6, s32[2048]{0:T(1024)S(1)} %get-tuple-element.5), kind=kCustom, calls=%fused_computation | custom fusion | bytes 33562624 | tf_op jit(solution)/shard_map/gather | solution.py:36
  47.8 194.3 %all_to_all.15 = bf16[32,2,32,4096]{3,2,1,0:T(8,128)(2,1)S(1)} all-to-all(bf16[32,2,32,4096]{3,2,1,0:T(8,128)(2,1)} %bitcast.54), channel_id=1, replica_groups=mesh['dp'=4,'expert'=32] {'expert'}, dimensions={0} | all-to-all | bytes 33554432 | tf_op jit(solution)/shard_map/all_to_all | solution.py:37
  242.1 12.0 %fusion.2 = f32[2,32,32,384]{3,2,1,0:T(8,128)} fusion(bf16[32,2,32,4096]{3,2,1,0:T(8,128)(2,1)S(1)} %all_to_all.15, bf16[2,4096,384]{2,1,0:T(8,128)(2,1)} %param.10), kind=kOutput, calls=%fused_computation.6 | convolution fusion | flops 6442450944 | bytes 26214400 | tf_op jit(solution)/shard_map/sxcd,xdf->xscf/dot_general | solution.py:38
  254.1 12.4 %multiply_convert_fusion = bf16[2,32,32,384]{3,2,1,0:T(8,128)(2,1)} fusion(f32[2,32,32,384]{3,2,1,0:T(8,128)} %fusion.2, bf16[2,4096,384]{2,1,0:T(8,128)(2,1)} %param.11, bf16[32,2,32,4096]{3,2,1,0:T(8,128)(2,1)S(1)} %all_to_all.15), kind=kOutput, calls=%fused_computation.18 | convolution fusion | flops 6447169536 | bytes 27787264 | tf_op jit(solution)/shard_map/sxcd,xdf->xscf/dot_general | solution.py:41
  266.5 0.0 all-gather.2.cloned.1.call-update
  266.5 67.6 %all-gather.2.cloned.1.call-done = bf16[2,32,32,1536]{3,2,1,0:T(8,128)(2,1)} async-done(((bf16[2,32,32,384]{3,2,1,0:T(8,128)(2,1)}), bf16[2,32,32,1536]{3,2,1,0:T(8,128)(2,1)}) %all-gather.2.cloned.1.call-update) | async-done | bytes 6291472 | tf_op jit(solution)/shard_map/all_gather | solution.py:43
  334.2 10.6 %convert_bitcast_fusion = bf16[32,2,32,1024]{3,2,0,1:T(8,128)(2,1)S(1)} fusion(bf16[2,32,32,1536]{3,2,1,0:T(8,128)(2,1)} %all-gather.2.cloned.1.call-done, bf16[2,1536,1024]{2,1,0:T(8,128)(2,1)} %param.12), kind=kOutput, calls=%fused_computation.17 | convolution fusion | flops 6444548096 | bytes 16777216 | tf_op jit(solution)/shard_map/xscf,xfd->sxcd/dot_general | solution.py:44
  344.8 2.5 copy.31
  347.2 0.0 copy-start.1
  347.2 7.8 %all-to-all-start.1 = ((bf16[32,2,32,1024]{3,2,1,0:T(8,128)(2,1)}), bf16[32,2,32,1024]{3,2,1,0:T(8,128)(2,1)}, u32[]{:S(2)}, u32[]{:S(2)}) async-start(bf16[32,2,32,1024]{3,2,1,0:T(8,128)(2,1)} %copy.31), calls=%async_computation.1 | async-start | bytes 8388608 | tf_op jit(solution)/shard_map/all_to_all | solution.py:47
  355.0 0.0 copy-done.1
  355.0 0.1 copy.29
  355.1 0.1 mul.70
  355.2 49.9 %all-to-all-done.1 = bf16[32,2,32,1024]{3,2,1,0:T(8,128)(2,1)} async-done(((bf16[32,2,32,1024]{3,2,1,0:T(8,128)(2,1)}), bf16[32,2,32,1024]{3,2,1,0:T(8,128)(2,1)}, u32[]{:S(2)}, u32[]{:S(2)}) %all-to-all-start.1) | async-done | bytes 4194336 | tf_op jit(solution)/shard_map/all_to_all | solution.py:47
  405.2 0.0 copy-start
  405.2 7.7 %gather_fusion.1 = bf16[1024,1024]{1,0:T(8,128)(2,1)S(1)} fusion(bf16[2048,1024]{1,0:T(8,128)(2,1)} %bitcast.12, s32[1024]{0:T(1024)S(1)} %broadcast_clamp_fusion), kind=kCustom, calls=%fused_computation.1 | custom fusion | bytes 4198400 | tf_op jit(solution)/shard_map/gather | solution.py:48
  412.9 1.3 fusion.8
  414.2 0.0 copy-done
  414.2 0.8 fusion.26
  415.0 0.3 bitcast_multiply_fusion
  415.3 0.2 concatenate.7
  415.5 9.6 %gather_fusion.2 = bf16[2048,1024]{1,0:T(8,128)(2,1)} fusion(bf16[1025,1024]{1,0:T(8,128)(2,1)S(1)} %concatenate.7, s32[2048]{0:T(1024)S(1)} %get-tuple-element.4), kind=kCustom, calls=%fused_computation.2 | custom fusion | bytes 8396800 | tf_op jit(solution)/shard_map/gather | solution.py:56
  425.1 58.3 %all_to_all.16 = bf16[32,2,32,1024]{3,2,1,0:T(8,128)(2,1)S(1)} all-to-all(bf16[32,2,32,1024]{3,2,1,0:T(8,128)(2,1)} %bitcast.55), channel_id=1, replica_groups=mesh['dp'=4,'expert'=32] {'expert'}, dimensions={0} | all-to-all | bytes 8388608 | tf_op jit(solution)/shard_map/all_to_all | solution.py:57
  483.4 11.5 %bitcast_convert_fusion = bf16[2,1536,1024]{2,1,0:T(8,128)(2,1)} fusion(bf16[2,32,32,1536]{3,2,1,0:T(8,128)(2,1)} %all-gather.2.cloned.1.call-done, bf16[32,2,32,1024]{3,2,1,0:T(8,128)(2,1)S(1)} %all_to_all.16), kind=kOutput, calls=%fused_computation.8 | convolution fusion | flops 6445596672 | bytes 16777216 | tf_op jit(solution)/shard_map/xscf,sxcd->xfd/dot_general | solution.py:58
  (7 shorter events, 0.1 us)
Async XLA Ops:
  7.2 327.0 %all-gather.2.cloned.1.call-start = ((), (), s32[]{:S(2)}) async-start(), calls=%async_computation.3 | async-start | bytes 7864320 | tf_op jit(solution)/shard_map/all_gather | solution.py:43
  347.2 7.8 %copy-start.1 = (f32[128,8]{0,1:T(8,128)S(1)}, f32[128,8]{0,1:T(8,128)}, u32[]{:S(2)}) copy-start(f32[128,8]{0,1:T(8,128)} %param.9) | copy-start | bytes 12292
  347.2 57.9 %all-to-all-start.1 = ((bf16[32,2,32,1024]{3,2,1,0:T(8,128)(2,1)}), bf16[32,2,32,1024]{3,2,1,0:T(8,128)(2,1)}, u32[]{:S(2)}, u32[]{:S(2)}) async-start(bf16[32,2,32,1024]{3,2,1,0:T(8,128)(2,1)} %copy.31), calls=%async_computation.1 | async-start | bytes 8388608 | tf_op jit(solution)/shard_map/all_to_all | solution.py:47
  405.2 9.0 %copy-start = (f32[1024]{0:T(1024)S(1)}, f32[1024]{0:T(1024)}, u32[]{:S(2)}) copy-start(f32[1024]{0:T(1024)} %param.13) | copy-start | bytes 12292
Sparse Core Ops, SparseCore 0:
  266.7 67.4 all-gather.1
where the time goes:
time: 502 us
  blocking collectives  253 us (50%)
  waiting for transfers between devices  118 us (24%)
  matrix products  46.6 us (9%)
  local copies, waits for them, and re-layouts  41.6 us (8%)
  other arithmetic  21.3 us (4%)
  between operations  14.2 us (3%)
  starting transfers between devices  7.81 us (2%)
    all_to_all x1, blocking collectives, per_device(): lax.all_to_all(outgoing, 'expert', split_axis=0, concat_axis=0, tiled=True)  194 us
    all_gather x1, waiting for transfers between devices, per_device(): hidden = lax.all_gather(hidden_share, 'dp', axis=3, tiled=True)  67.6 us
    all_to_all x1, blocking collectives, per_device(): lax.all_to_all(outgoing_scaled, 'expert', split_axis=0, concat_axis=0, ti...  58.3 us
    all_to_all x1, waiting for transfers between devices, per_device(): lax.all_to_all(expert_out, 'expert', split_axis=0, concat_axis=0, tiled=T...  49.9 us
    another operation x3, other arithmetic  18.2 us
    gather x1, local copies, waits for them, and re-layouts, per_device(): outgoing = padded[owner_tokens].reshape(shape_out + (width,))  14.3 us
    dot_general x1, matrix products, per_device(): jnp.einsum('sxcd,xdf->xscf', arrived, up_weight, preferred_element_type=j...  12.4 us
    dot_general x1, matrix products, per_device(): jnp.einsum('sxcd,xdf->xscf', arrived, gate_weight, preferred_element_type...  12 us
  transfers between devices with their start and end apart: 2, of which 2 were waited for; matrix products, arithmetic and copies ran while one was open for 0% of the time, Pallas kernels for 0%

commit v1 on v0

--- a/solution.py
+++ b/solution.py
@@ -2,6 +2,18 @@
 import jax.numpy as jnp
 from jax import lax
 from jax.sharding import PartitionSpec as P
+
+
+def doubled_up(x, axis, dim):
+    ways, here, turn = (lax.axis_size(axis), lax.axis_index(axis), x.shape[dim])
+    line, have = (x, 1)
+    while have < ways:
+        line = jnp.concatenate(
+            [line, lax.ppermute(line, axis, [(d, (d - have) % ways) for d in range(ways)])],
+            axis=dim,
+        )
+        have = 2 * have
+    return jnp.roll(line, here * turn, axis=dim)
 
 
 def slot_of_rows(flat_ids, expert_total, capacity):
@@ -40,7 +52,7 @@
     )
     up_pre = jnp.einsum("sxcd,xdf->xscf", arrived, up_weight, preferred_element_type=jnp.float32)
     hidden_share = (jax.nn.silu(gate_pre) * up_pre).astype(jnp.bfloat16)
-    hidden = lax.all_gather(hidden_share, "dp", axis=3, tiled=True)
+    hidden = doubled_up(hidden_share, "dp", 3)
     expert_out = jnp.einsum(
         "xscf,xfd->sxcd", hidden, tangent, preferred_element_type=jnp.float32
     ).astype(jnp.bfloat16)

time: 502 us -> 553 us (1.10)
  waiting for transfers between devices: 118 us -> 150 us
  local copies, waits for them, and re-layouts: 41.6 us -> 59.7 us
  between operations: 14.2 us -> 0.8 us
  starting transfers between devices: 7.81 us -> 14.3 us
    ppermute x0 -> x2, waiting for transfers between devices: none -> 99.9 us  [doubled_up(): lax.ppermute(line, axis, [(d, (d - have) % ways) for d in range(ways)])]
    all_gather x1 -> x0, waiting for transfers between devices: 67.6 us -> none  [per_device(): hidden = lax.all_gather(hidden_share, 'dp', axis=3, tiled=True)]
    unnamed x6 -> x16, local copies, waits for them, and re-layouts: 0.9 us -> 15.1 us
    ppermute x0 -> x2, starting transfers between devices: none -> 5.8 us  [doubled_up(): lax.ppermute(line, axis, [(d, (d - have) % ways) for d in range(ways)])]
  transfers between devices with their start and end apart: 2 -> 3, of which waited for: 2 -> 3; matrix products, arithmetic and copies ran while one was open for 0% -> 0% of each run, Pallas kernels for 0% -> 0%
where the time goes in v1:
time: 553 us
  blocking collectives  253 us (46%)
  waiting for transfers between devices  150 us (27%)
  local copies, waits for them, and re-layouts  59.7 us (11%)
  matrix products  51.9 us (9%)
  other arithmetic  23.5 us (4%)
  starting transfers between devices  14.3 us (3%)
    all_to_all x1, blocking collectives, per_device(): lax.all_to_all(outgoing, 'expert', split_axis=0, concat_axis=0, tiled=True)  194 us
    ppermute x2, waiting for transfers between devices, doubled_up(): lax.ppermute(line, axis, [(d, (d - have) % ways) for d in range(ways)])  99.9 us
    all_to_all x1, blocking collectives, per_device(): lax.all_to_all(outgoing_scaled, 'expert', split_axis=0, concat_axis=0, ti...  58.2 us
    all_to_all x1, waiting for transfers between devices, per_device(): lax.all_to_all(expert_out, 'expert', split_axis=0, concat_axis=0, tiled=T...  50 us
    another operation x3, other arithmetic  18.2 us
    dot_general x1, matrix products, per_device(): jnp.einsum('sxcd,xdf->xscf', arrived, up_weight, preferred_element_type=j...  15.7 us
    dot_general x1, matrix products, per_device(): jnp.einsum('xscf,sxcd->xfd', hidden, incoming, preferred_element_type=jnp...  15.2 us
    unnamed x16, local copies, waits for them, and re-layouts  15.1 us
  transfers between devices with their start and end apart: 3, of which 3 were waited for; matrix products, arithmetic and copies ran while one was open for 0% of the time, Pallas kernels for 0%

profile of v1, /device:TPU:1, one launch (start us, length us, event | category | flops | bytes accessed | tf_op | source)
XLA Modules:
  0.0 552.6 jit_solution(9747372162353329240)
XLA Ops:
  0.6 0.8 copy.23
  1.4 0.1 eq.32
  1.5 0.1 eq.28
  1.6 0.7 broadcast_multiply_fusion.1
  2.3 18.0 %reduce-window.6 = s32[64,8,128]{2,1,0:T(8,128)S(1)} reduce-window(s32[64,8,128]{2,1,0:T(8,128)S(1)} %fusion.23, s32[]{:T(128)} %constant.52.clone.1), window={size=1x1x128 pad=0_0x0_0x127_0}, to_apply=%region_0.0 | reduce-window | flops 8323072 | bytes 524292 | tf_op jit(solution)/shard_map/reduce-window
  20.3 0.1 slice.14
  20.5 0.1 copy.25
  20.6 0.1 copy.26
  20.7 0.1 broadcast_add_fusion
  20.9 0.1 copy.22
  21.0 0.1 mul.69
  21.1 0.1 fusion.22
  21.2 4.3 scatter_custom_fusion
  25.5 1.3 concatenate.16
  26.9 14.3 %gather_fusion = bf16[2048,4096]{1,0:T(8,128)(2,1)} fusion(bf16[129,4096]{1,0:T(8,128)(2,1)S(1)} %concatenate.16, s32[2048]{0:T(1024)S(1)} %get-tuple-element.5), kind=kCustom, calls=%fused_computation | custom fusion | bytes 33562624 | tf_op jit(solution)/shard_map/gather | solution.py:48
  41.1 194.3 %all_to_all.15 = bf16[32,2,32,4096]{3,2,1,0:T(8,128)(2,1)S(1)} all-to-all(bf16[32,2,32,4096]{3,2,1,0:T(8,128)(2,1)} %bitcast.54), channel_id=1, replica_groups=mesh['dp'=4,'expert'=32] {'expert'}, dimensions={0} | all-to-all | bytes 33554432 | tf_op jit(solution)/shard_map/all_to_all | solution.py:49
  235.4 0.0 copy-start
  235.4 5.7 %copy-done = bf16[32,2,32,4096]{3,2,1,0:T(8,128)(2,1)} copy-done((bf16[32,2,32,4096]{3,2,1,0:T(8,128)(2,1)}, bf16[32,2,32,4096]{3,2,1,0:T(8,128)(2,1)S(1)}, u32[]{:S(2)}) %copy-start) | copy-done | bytes 16777240
  241.2 12.0 %fusion.2 = f32[2,32,32,384]{3,2,1,0:T(8,128)} fusion(bf16[32,2,32,4096]{3,2,1,0:T(8,128)(2,1)S(1)} %all_to_all.15, bf16[2,4096,384]{2,1,0:T(8,128)(2,1)} %param.10), kind=kOutput, calls=%fused_computation.6 | convolution fusion | flops 6442450944 | bytes 26214400 | tf_op jit(solution)/shard_map/sxcd,xdf->xscf/dot_general | solution.py:50
  253.2 15.7 %constant_dynamic-update-slice_fusion.5 = (bf16[2,32,32,3072]{3,2,1,0:T(8,128)(2,1)}, bf16[2,32,32,384]{3,2,1,0:T(8,128)(2,1)S(1)}) fusion(bf16[2,4096,384]{2,1,0:T(8,128)(2,1)} %param.11, bf16[32,2,32,4096]{3,2,1,0:T(8,128)(2,1)} %copy-done, f32[2,32,32,384]{3,2,1,0:T(8,128)} %fusion.2), kind=kOutput, calls=%fused_computation.38 | convolution fusion | flops 6447169536 | bytes 29360128 | tf_op jit(solution)/shard_map/sxcd,xdf->xscf/dot_general | solution.py:53
  268.9 3.8 collective-permute-start
  272.6 33.4 %collective-permute-done = bf16[2,32,32,384]{3,2,1,0:T(8,128)(2,1)S(1)} collective-permute-done((bf16[2,32,32,384]{3,2,1,0:T(8,128)(2,1)S(1)}, bf16[2,32,32,384]{3,2,1,0:T(8,128)(2,1)S(1)}, u32[]{:S(2)}, u32[]{:S(2)}) %collective-permute-start) | collective-permute-done | bytes 1572896 | tf_op jit(solution)/shard_map/ppermute | solution.py:12
  306.0 2.1 pad_maximum_fusion
  308.1 2.0 collective-permute-start.1
  310.2 1.6 constant_dynamic-update-slice_fusion.4
  311.8 66.5 %collective-permute-done.1 = bf16[2,32,32,768]{3,2,1,0:T(8,128)(2,1)} collective-permute-done((bf16[2,32,32,768]{3,2,1,0:T(8,128)(2,1)}, bf16[2,32,32,768]{3,2,1,0:T(8,128)(2,1)}, u32[]{:S(2)}, u32[]{:S(2)}) %collective-permute-start.1) | collective-permute-done | bytes 3145760 | tf_op jit(solution)/shard_map/ppermute | solution.py:12
  378.3 0.0 slice-start
  378.3 4.0 constant_dynamic-update-slice_fusion.3
  382.3 1.4 constant_dynamic-update-slice_fusion.2
  383.8 0.0 slice-start.1
  383.8 1.4 constant_dynamic-update-slice_fusion.1
  385.2 3.9 constant_dynamic-update-slice_fusion
  389.1 0.0 slice-done
  389.1 0.0 slice-done.1
  389.1 8.9 %convert_bitcast_fusion = bf16[32,2,32,1024]{3,2,0,1:T(8,128)(2,1)S(1)} fusion(bf16[2,1536,1024]{2,1,0:T(8,128)(2,1)S(1)} %bitcast.62, bf16[2,32,32,3072]{3,2,1,0:T(8,128)(2,1)} %constant_dynamic-update-slice_fusion, s32[]{:T(128)S(6)} %select_n.39), kind=kOutput, calls=%fused_computation.19 | convolution fusion | flops 6444548096 | bytes 16777220 | tf_op jit(solution)/shard_map/xscf,xfd->sxcd/dot_general | solution.py:56
  398.1 2.5 copy.31
  400.5 0.0 copy-start.2
  400.5 8.5 %all-to-all-start.1 = ((bf16[32,2,32,1024]{3,2,1,0:T(8,128)(2,1)}), bf16[32,2,32,1024]{3,2,1,0:T(8,128)(2,1)}, u32[]{:S(2)}, u32[]{:S(2)}) async-start(bf16[32,2,32,1024]{3,2,1,0:T(8,128)(2,1)} %copy.31), calls=%async_computation.1 | async-start | bytes 8388608 | tf_op jit(solution)/shard_map/all_to_all | solution.py:59
  409.0 0.0 copy-done.2
  409.0 0.1 copy.29
  409.1 0.1 mul.74
  409.2 50.0 %all-to-all-done.1 = bf16[32,2,32,1024]{3,2,1,0:T(8,128)(2,1)} async-done(((bf16[32,2,32,1024]{3,2,1,0:T(8,128)(2,1)}), bf16[32,2,32,1024]{3,2,1,0:T(8,128)(2,1)}, u32[]{:S(2)}, u32[]{:S(2)}) %all-to-all-start.1) | async-done | bytes 4194336 | tf_op jit(solution)/shard_map/all_to_all | solution.py:59
  459.3 0.0 copy-start.1
  459.3 7.7 %gather_fusion.1 = bf16[1024,1024]{1,0:T(8,128)(2,1)S(1)} fusion(bf16[2048,1024]{1,0:T(8,128)(2,1)} %bitcast.12, s32[1024]{0:T(1024)S(1)} %broadcast_clamp_fusion), kind=kCustom, calls=%fused_computation.1 | custom fusion | bytes 4198400 | tf_op jit(solution)/shard_map/gather | solution.py:60
  467.0 1.3 fusion.10
  468.3 0.0 copy-done.1
  468.3 0.8 fusion.32
  469.1 0.3 bitcast_multiply_fusion
  469.4 0.2 concatenate.19
  469.6 9.6 %gather_fusion.2 = bf16[2048,1024]{1,0:T(8,128)(2,1)} fusion(bf16[1025,1024]{1,0:T(8,128)(2,1)S(1)} %concatenate.19, s32[2048]{0:T(1024)S(1)} %get-tuple-element.4), kind=kCustom, calls=%fused_computation.2 | custom fusion | bytes 8396800 | tf_op jit(solution)/shard_map/gather | solution.py:68
  479.2 58.2 %all_to_all.16 = bf16[32,2,32,1024]{3,2,1,0:T(8,128)(2,1)S(1)} all-to-all(bf16[32,2,32,1024]{3,2,1,0:T(8,128)(2,1)} %bitcast.55), channel_id=1, replica_groups=mesh['dp'=4,'expert'=32] {'expert'}, dimensions={0} | all-to-all | bytes 8388608 | tf_op jit(solution)/shard_map/all_to_all | solution.py:69
  537.4 15.2 %bitcast_convert_fusion = bf16[2,1536,1024]{2,1,0:T(8,128)(2,1)} fusion(bf16[2,32,32,3072]{3,2,1,0:T(8,128)(2,1)} %constant_dynamic-update-slice_fusion, s32[]{:T(128)S(6)} %select_n.39, bf16[32,2,32,1024]{3,2,1,0:T(8,128)(2,1)S(1)} %all_to_all.16), kind=kOutput, calls=%fused_computation.8 | convolution fusion | flops 6445596672 | bytes 16777220 | tf_op jit(solution)/shard_map/xscf,sxcd->xfd/dot_general | solution.py:70
  (8 shorter events, 0.1 us)
Async XLA Ops:
  235.4 5.7 %copy-start = (bf16[32,2,32,4096]{3,2,1,0:T(8,128)(2,1)}, bf16[32,2,32,4096]{3,2,1,0:T(8,128)(2,1)S(1)}, u32[]{:S(2)}) copy-start(bf16[32,2,32,4096]{3,2,1,0:T(8,128)(2,1)S(1)} %all_to_all.15) | copy-start | bytes 50331652
  268.9 37.1 %collective-permute-start = (bf16[2,32,32,384]{3,2,1,0:T(8,128)(2,1)S(1)}, bf16[2,32,32,384]{3,2,1,0:T(8,128)(2,1)S(1)}, u32[]{:S(2)}, u32[]{:S(2)}) collective-permute-start(bf16[2,32,32,384]{3,2,1,0:T(8,128)(2,1)S(1)} %get-tuple-element.7), channel_id=1, source_target_pairs={{0,96},{32,0},{64,32},{96,64},{1,97},{33,1},{65,33},{97,65},{2,98}... | collective-permute-start | bytes 4718600 | tf_op jit(solution)/shard_map/ppermute | solution.py:12
  308.1 70.2 %collective-permute-start.1 = (bf16[2,32,32,768]{3,2,1,0:T(8,128)(2,1)}, bf16[2,32,32,768]{3,2,1,0:T(8,128)(2,1)}, u32[]{:S(2)}, u32[]{:S(2)}) collective-permute-start(bf16[2,32,32,768]{3,2,1,0:T(8,128)(2,1)} %pad_maximum_fusion), channel_id=1, source_target_pairs={{0,64},{32,96},{64,0},{96,32},{1,65},{33,97},{65,1},{97,33},{2,66}... | collective-permute-start | bytes 9437192 | tf_op jit(solution)/shard_map/ppermute | solution.py:12
  378.3 10.8 %slice-start = ((s8[6291456]{0:T(1024)(128)(4,1)}), s8[4194304]{0:T(1024)(128)(4,1)S(1)}, s32[]{:S(2)}) async-start(s8[6291456]{0:T(1024)(128)(4,1)} %bitcast.61), calls=%async_computation.3 | async-start | bytes 8388608
  383.8 5.3 slice-start.1
  400.5 8.5 %copy-start.2 = (f32[128,8]{0,1:T(8,128)S(1)}, f32[128,8]{0,1:T(8,128)}, u32[]{:S(2)}) copy-start(f32[128,8]{0,1:T(8,128)} %param.9) | copy-start | bytes 12292
  400.5 58.8 %all-to-all-start.1 = ((bf16[32,2,32,1024]{3,2,1,0:T(8,128)(2,1)}), bf16[32,2,32,1024]{3,2,1,0:T(8,128)(2,1)}, u32[]{:S(2)}, u32[]{:S(2)}) async-start(bf16[32,2,32,1024]{3,2,1,0:T(8,128)(2,1)} %copy.31), calls=%async_computation.1 | async-start | bytes 8388608 | tf_op jit(solution)/shard_map/all_to_all | solution.py:59
  459.3 9.0 %copy-start.1 = (f32[1024]{0:T(1024)S(1)}, f32[1024]{0:T(1024)}, u32[]{:S(2)}) copy-start(f32[1024]{0:T(1024)} %param.13) | copy-start | bytes 12292
